TPU v7x, 256 devices: a whole 4x4x8 slice. The times are simulated.
256 devices in a mesh: pair: 32 (over z, y), cd: 8 (over x, core).
Axes of the slice: x: 4, y: 4, z: 8, core: 2. Of those that a mesh axis runs over, the one named last changes fastest.
Arguments:
- amplitudes: bfloat16 [8192, 4096], P('pair', 'cd'), may hold values from -6 to 6
- integrals: bfloat16 [2, 8192, 4096], P(None, 'pair', 'cd'), may hold values from -0.1875 to 0.1875
- row_irreps: int32 [32, 2], P('pair'), may hold values from 0 to 3
- col_irreps: int32 [16, 2], P('cd'), may hold values from 0 to 3
Outputs:
- sigma: bfloat16 [8192, 8192], P('cd', 'pair')
All inputs are finite; a program needn't handle non-finite values.
Results may differ from a plain program's by a relative error of at most 0.014.
Values may be sent and summed in bfloat16 or wider, within the bound.
A program may use at most 192 MiB of HBM per device.

v0:
```python
import jax
import jax.numpy as jnp
from jax import lax
from jax.sharding import PartitionSpec as P


def pair_symmetry(labels):
    return jnp.bitwise_xor(labels[:, 0], labels[:, 1])


def tile_product(left_part, right_part):
    return lax.dot_general(
        left_part, right_part, (((1,), (1,)), ((), ())), preferred_element_type=jnp.float32
    )


def on_device(amplitudes, integrals, row_irreps, col_irreps):
    row_tiles = row_irreps.shape[0]
    col_tiles = col_irreps.shape[0]
    tile_size = integrals.shape[1] // row_tiles
    allowed = pair_symmetry(row_irreps)[:, None] == pair_symmetry(col_irreps)[None, :]
    raw_rows = lax.all_gather(amplitudes, "pair", axis=0, tiled=True)
    middle = raw_rows.shape[0] // 2
    direct = raw_rows[:middle].astype(jnp.float32)
    mirrored = raw_rows[middle:].astype(jnp.float32)
    gathered = jnp.concatenate([direct + mirrored, direct - mirrored], 0).astype(jnp.bfloat16)
    half_rows = gathered.shape[0] // 2
    shard_rows = gathered.shape[0] // lax.axis_size("cd")
    weight_mask = allowed.astype(jnp.bfloat16)
    shaped = (
        integrals.reshape(2, row_tiles, tile_size, col_tiles, tile_size)
        * weight_mask[None, :, None, :, None]
    )
    weights = shaped.reshape(integrals.shape)

    def contract(row_block, channel_weights):
        return tile_product(row_block, channel_weights)

    first_index = jnp.int32(0)
    pieces = []
    for number in range(shard_rows * lax.axis_size("cd") // shard_rows):
        first_row = first_index + number * shard_rows
        upper = (first_row >= half_rows).astype(jnp.int32)
        local_row = first_row - upper * half_rows
        plus_rows = lax.dynamic_slice_in_dim(gathered, local_row, shard_rows, 0)
        minus_rows = lax.dynamic_slice_in_dim(gathered, local_row + half_rows, shard_rows, 0)
        plus_term = contract(plus_rows, weights[0])
        minus_term = contract(minus_rows, weights[1])
        factor = 1.0 - 2.0 * upper.astype(jnp.float32)
        pieces.append(plus_term + factor * minus_term)
    return lax.psum_scatter(
        jnp.concatenate(pieces, 0).astype(jnp.bfloat16), "cd", scatter_dimension=0, tiled=True
    )


def solution(mesh):
    in_specs = (P("pair", "cd"), P(None, "pair", "cd"), P("pair", None), P("cd", None))
    out_specs = P("cd", "pair")
    return jax.shard_map(
        on_device, mesh=mesh, in_specs=in_specs, out_specs=out_specs, check_vma=False
    )
```

profile of v0, /device:TPU:8, one launch (start us, length us, event | category | flops | bytes accessed | tf_op | source)
XLA Modules:
  0.0 171.2 jit_solution(2034880087262283231)
XLA Ops:
  6.5 0.0 all-gather.2.cloned.1.call-start
  6.5 0.7 all-gather.2.cloned.1.call-update
  7.3 0.0 reduce-scatter.2.cloned.1.call-start
  7.3 1.2 reshape.47
  8.5 1.3 fusion.28
  11.1 0.9 fusion.26
  12.1 0.5 broadcast_multiply_fusion
  12.6 0.4 fusion.27
  13.0 97.1 %all-gather.2.cloned.1.call-done = bf16[8192,512]{1,0:T(8,128)(2,1)} async-done(((bf16[256,512]{1,0:T(8,128)(2,1)}), bf16[8192,512]{1,0:T(8,128)(2,1)}) %all-gather.2.cloned.1.call-update) | async-done | bytes 8388624 | tf_op jit(solution)/shard_map/all_gather | solution.py:22
  110.1 4.4 %fusion.1 = (bf16[4096,512]{1,0:T(8,128)(2,1)S(1)}, bf16[4096,512]{1,0:T(8,128)(2,1)S(1)}) fusion(bf16[8192,512]{1,0:T(8,128)(2,1)} %all-gather.2.cloned.1.call-done), kind=kLoop, calls=%fused_computation.3 | loop fusion | flops 12582912 | bytes 16777216 | tf_op jit(solution)/shard_map/convert.10
  114.6 0.5 fusion.2
  115.0 0.5 fusion.6
  115.5 0.5 fusion.10
  116.0 0.5 fusion.14
  116.4 1.3 fusion.18
  117.7 1.3 fusion.19
  119.0 1.3 fusion.20
  120.3 1.3 fusion.21
  121.6 0.9 fusion.22
  122.5 1.0 fusion.23
  123.5 0.9 fusion.24
  124.4 0.9 fusion.25
  125.3 0.0 reduce-scatter.2.cloned.1.call-update
  125.3 39.0 %reduce-scatter.2.cloned.1.call-done = bf16[1024,256]{1,0:T(8,128)(2,1)} async-done(((bf16[8192,256]{1,0:T(8,128)(2,1)}), bf16[1024,256]{1,0:T(8,128)(2,1)}) %reduce-scatter.2.cloned.1.call-update) | async-done | bytes 524304 | tf_op jit(solution)/shard_map/reduce_scatter | solution.py:51
  (2 shorter events, 0.1 us)
Async XLA Ops:
  6.5 103.6 %all-gather.2.cloned.1.call-start = ((), (), s32[]{:S(2)}) async-start(), calls=%async_computation.1 | async-start | bytes 8650752 | tf_op jit(solution)/shard_map/all_gather | solution.py:22
  7.3 157.1 %reduce-scatter.2.cloned.1.call-start = ((), (), s32[]{:S(2)}) async-start(), calls=%async_computation.2 | async-start | bytes 4718592 | tf_op jit(solution)/shard_map/reduce_scatter | solution.py:51
Sparse Core Ops, SparseCore 0:
  9.9 100.1 all-gather.1
  125.5 38.8 reduce-scatter.1
where the time goes:
time: 171 us
  waiting for transfers between devices  137 us (80%)
  between operations  14.8 us (9%)
  other arithmetic  9.62 us (6%)
  matrix products  6.97 us (4%)
  local copies, waits for them, and re-layouts  2.91 us (2%)
    all_gather x1, waiting for transfers between devices, on_device(): raw_rows = lax.all_gather(amplitudes, 'pair', axis=0, tiled=True)  97.1 us
    reduce_scatter x1, waiting for transfers between devices, on_device(): lax.psum_scatter(jnp.concatenate(pieces, 0).astype(jnp.bfloat16), 'cd', s...  39 us
    dot_general x8, matrix products, tile_product(): lax.dot_general(left_part, right_part, (((1,), (1,)), ((), ())), preferre...  6.97 us
    another operation x1, other arithmetic  4.4 us
  transfers between devices with their start and end apart: 2, of which 2 were waited for; matrix products, arithmetic and copies ran while one was open for 3% of the time, Pallas kernels for 0%

commit v1 on v0

--- a/solution.py
+++ b/solution.py
@@ -19,7 +19,9 @@
     col_tiles = col_irreps.shape[0]
     tile_size = integrals.shape[1] // row_tiles
     allowed = pair_symmetry(row_irreps)[:, None] == pair_symmetry(col_irreps)[None, :]
-    raw_rows = lax.all_gather(amplitudes, "pair", axis=0, tiled=True)
+    raw_rows = jnp.concatenate(
+        lax.all_to_all(jnp.stack([amplitudes] * lax.axis_size("pair")), "pair", 0, 0), axis=0
+    )
     middle = raw_rows.shape[0] // 2
     direct = raw_rows[:middle].astype(jnp.float32)
     mirrored = raw_rows[middle:].astype(jnp.float32)

time: 171 us -> 282 us (1.65)
  waiting for transfers between devices: 137 us -> 232 us
  starting transfers between devices: 0.04 us -> 11.9 us
  local copies, waits for them, and re-layouts: 2.91 us -> 6.94 us
    all_to_all x0 -> x1, waiting for transfers between devices: none -> 187 us  [on_device(): lax.all_to_all(jnp.stack([amplitudes] * lax.axis_size('pair')), 'pair', 0...]
    all_gather x1 -> x0, waiting for transfers between devices: 97.1 us -> none  [on_device(): raw_rows = lax.all_gather(amplitudes, 'pair', axis=0, tiled=True)]
    all_to_all x0 -> x1, starting transfers between devices: none -> 11.9 us  [on_device(): lax.all_to_all(jnp.stack([amplitudes] * lax.axis_size('pair')), 'pair', 0...]
    reduce_scatter x1, waiting for transfers between devices: 39 us -> 45.5 us  [on_device(): lax.psum_scatter(jnp.concatenate(pieces, 0).astype(jnp.bfloat16), 'cd', s...]
    another operation x0 -> x1, local copies, waits for them, and re-layouts: none -> 5.14 us  [on_device(): jnp.stack([amplitudes] * lax.axis_size('pair'))]
  transfers between devices with their start and end apart: 2 -> 2, of which waited for: 2 -> 2; matrix products, arithmetic and copies ran while one was open for 3% -> 1% of each run, Pallas kernels for 0% -> 0%
where the time goes in v1:
time: 282 us
  waiting for transfers between devices  232 us (82%)
  between operations  14.8 us (5%)
  starting transfers between devices  11.9 us (4%)
  other arithmetic  8.93 us (3%)
  matrix products  7.01 us (2%)
  local copies, waits for them, and re-layouts  6.94 us (2%)
    all_to_all x1, waiting for transfers between devices, on_device(): lax.all_to_all(jnp.stack([amplitudes] * lax.axis_size('pair')), 'pair', 0...  187 us
    reduce_scatter x1, waiting for transfers between devices, on_device(): lax.psum_scatter(jnp.concatenate(pieces, 0).astype(jnp.bfloat16), 'cd', s...  45.5 us
    all_to_all x1, starting transfers between devices, on_device(): lax.all_to_all(jnp.stack([amplitudes] * lax.axis_size('pair')), 'pair', 0...  11.9 us
    dot_general x8, matrix products, tile_product(): lax.dot_general(left_part, right_part, (((1,), (1,)), ((), ())), preferre...  7.01 us
  transfers between devices with their start and end apart: 2, of which 2 were waited for; matrix products, arithmetic and copies ran while one was open for 1% of the time, Pallas kernels for 0%

profile of v1, /device:TPU:8, one launch (start us, length us, event | category | flops | bytes accessed | tf_op | source)
XLA Modules:
  0.0 281.6 jit_solution(4351099025780105987)
XLA Ops:
  6.5 5.1 %stack.2 = bf16[32,256,512]{2,1,0:T(8,128)(2,1)} broadcast(bf16[256,512]{1,0:T(8,128)(2,1)} %param.4), dimensions={1,2} | broadcast | bytes 8650752 | tf_op jit(solution)/shard_map/stack | solution.py:23
  11.7 0.0 copy-start
  11.7 0.0 copy-start.2
  11.7 0.0 copy-start.1
  11.7 11.9 %all-to-all-start = ((bf16[32,256,512]{2,1,0:T(8,128)(2,1)}), bf16[32,256,512]{2,1,0:T(8,128)(2,1)}, u32[]{:S(2)}, u32[]{:S(2)}) async-start(bf16[32,256,512]{2,1,0:T(8,128)(2,1)} %stack.2), calls=%async_computation | async-start | bytes 16777216 | tf_op jit(solution)/shard_map/all_to_all | solution.py:23
  23.6 0.0 reduce-scatter.2.cloned.1.call-start
  23.6 0.0 copy-done
  23.6 0.1 reshape.66
  23.8 0.0 copy-done.2
  23.8 0.6 fusion.14
  25.6 0.0 copy-done.1
  25.6 0.2 fusion.10
  25.8 0.5 broadcast_multiply_fusion
  26.4 0.4 fusion.13
  26.8 186.5 %all-to-all-done = bf16[32,256,512]{2,1,0:T(8,128)(2,1)} async-done(((bf16[32,256,512]{2,1,0:T(8,128)(2,1)}), bf16[32,256,512]{2,1,0:T(8,128)(2,1)}, u32[]{:S(2)}, u32[]{:S(2)}) %all-to-all-start) | async-done | bytes 8388640 | tf_op jit(solution)/shard_map/all_to_all | solution.py:23
  213.3 4.4 %fusion.1 = (bf16[16,256,512]{2,1,0:T(8,128)(2,1)S(1)}, bf16[16,256,512]{2,1,0:T(8,128)(2,1)S(1)}) fusion(bf16[32,256,512]{2,1,0:T(8,128)(2,1)} %all-to-all-done), kind=kLoop, calls=%fused_computation.3 | loop fusion | flops 12582912 | bytes 16777216 | tf_op jit(solution)/shard_map/convert.11
  217.7 0.7 fusion.11
  218.4 0.5 fusion.18
  218.9 0.5 fusion.17
  219.3 0.5 fusion.16
  219.8 0.5 fusion.15
  220.3 1.3 fusion.2
  221.5 1.3 fusion.3
  222.8 1.3 fusion.4
  224.1 1.3 fusion.5
  225.4 1.0 fusion.6
  226.4 1.0 fusion.7
  227.3 1.0 fusion.8
  228.3 0.9 fusion.9
  229.2 0.0 reduce-scatter.2.cloned.1.call-update
  229.3 45.5 %reduce-scatter.2.cloned.1.call-done = bf16[1024,256]{1,0:T(8,128)(2,1)} async-done(((bf16[8192,256]{1,0:T(8,128)(2,1)}), bf16[1024,256]{1,0:T(8,128)(2,1)}) %reduce-scatter.2.cloned.1.call-update) | async-done | bytes 524304 | tf_op jit(solution)/shard_map/reduce_scatter | solution.py:53
  (2 shorter events, 0.1 us)
Async XLA Ops:
  11.7 12.0 %copy-start = (bf16[2,256,512]{2,1,0:T(8,128)(2,1)S(1)}, bf16[2,256,512]{2,1,0:T(8,128)(2,1)}, u32[]{:S(2)}) copy-start(bf16[2,256,512]{2,1,0:T(8,128)(2,1)} %param.5) | copy-start | bytes 1572868
  11.7 12.1 %copy-start.2 = (s32[1,2]{1,0:T(1,128)S(1)}, s32[1,2]{1,0:T(1,128)}, u32[]{:S(2)}) copy-start(s32[1,2]{1,0:T(1,128)} %param.6) | copy-start | bytes 28
  11.7 14.0 %copy-start.1 = (s32[2,2]{1,0:T(2,128)S(1)}, s32[2,2]{1,0:T(2,128)}, u32[]{:S(2)}) copy-start(s32[2,2]{1,0:T(2,128)} %param.7) | copy-start | bytes 52
  11.7 201.6 %all-to-all-start = ((bf16[32,256,512]{2,1,0:T(8,128)(2,1)}), bf16[32,256,512]{2,1,0:T(8,128)(2,1)}, u32[]{:S(2)}, u32[]{:S(2)}) async-start(bf16[32,256,512]{2,1,0:T(8,128)(2,1)} %stack.2), calls=%async_computation | async-start | bytes 16777216 | tf_op jit(solution)/shard_map/all_to_all | solution.py:23
  23.6 251.2 %reduce-scatter.2.cloned.1.call-start = ((), (), s32[]{:S(2)}) async-start(), calls=%async_computation.2 | async-start | bytes 4718592 | tf_op jit(solution)/shard_map/reduce_scatter | solution.py:53
Sparse Core Ops, SparseCore 0:
  229.4 45.3 reduce-scatter.1
